TPU v7x, 32 devices: a whole 2x2x4 slice. The times are simulated.
32 devices in a mesh: groups: 2 (over x), tm: 16 (over z, y, core).
Axes of the slice: x: 2, y: 2, z: 4, core: 2. Of those that a mesh axis runs over, the one named last changes fastest.
Arguments:
- process_noise: bfloat16 [1024, 64, 1024], P(('groups', 'tm')), parts along dimension 0, may hold values from -6 to 6
- gauge_reads: bfloat16 [1024, 96, 1024], P(('groups', 'tm')), parts along dimension 0, may hold values from -6 to 6
- sensor_active: int32 [1024, 96], P(('groups', 'tm')), parts along dimension 0, may hold values 0 or 1
- sensor_link: int32 [96], replicated, may hold values from 0 to 31
- reflectors: float32 [8, 64], P('groups'), parts along dimension 0, may hold values from -6 to 6
- decay_rates: float32 [64], P('groups'), parts along dimension 0, may hold values from 9.765625e-05 to 0.04
- turn_angles: float32 [64], P('groups'), parts along dimension 0, may hold values from -3.140625 to 3.140625
- gauge_gain: float32 [128], P('groups'), parts along dimension 0, may hold values from 0.01 to 0.05
Outputs:
- smoothed: float32 [1024, 64, 1024], P(('groups', 'tm')), parts along dimension 0
There are 2 independent parts, one for each index of `groups`. A program takes and returns all parts, laid end to end along the dimension named above; an argument that names none is the same for every part. Nothing has to cross between parts.
All inputs are finite; a program needn't handle non-finite values. No bound on the sum of `sensor_active` on one device may be relied on, other than what follows from the above.
Results may differ from a plain program's by a relative error of at most 0.0038.
Values sent between devices are 32-bit elements; how exact they have to be, the bound alone decides.
A program may use at most 128 MiB of HBM per device.

v0:
```python
import jax
import jax.numpy as jnp
from jax import lax
from jax.experimental import pallas as pl
from jax.experimental.pallas import tpu as pltpu
from jax.sharding import PartitionSpec as P

exact_mode = lax.Precision.HIGHEST
bf16 = jnp.bfloat16
f32 = jnp.float32


def rotation_basis(reflectors):
    width_all = reflectors.shape[1]
    rotation = jnp.eye(width_all, dtype=f32)
    for number in range(reflectors.shape[0]):
        vector = reflectors[number]
        factor = 2.0 / (jnp.sum(vector * vector) + 1e-06)
        rotation = rotation - factor * jnp.outer(
            jnp.dot(rotation, vector, precision=exact_mode), vector
        )
    return rotation


def pair_blocks(decay_rates, turn_angles):
    radius = jnp.exp(-decay_rates)
    cosine = jnp.repeat(radius * jnp.cos(turn_angles), 2)
    sine_part = jnp.repeat(radius * jnp.sin(turn_angles), 2)
    positions = jnp.arange(cosine.shape[0])
    pair_index = positions // 2
    parity = positions % 2
    same_pair = pair_index[:, None] == pair_index[None, :]
    same_parity = parity[:, None] == parity[None, :]
    upper = parity[:, None] == 0
    element = jnp.where(
        same_parity, cosine[:, None], jnp.where(upper, -sine_part[:, None], sine_part[:, None])
    )
    return jnp.where(same_pair, element, 0.0)


def two_parts(x):
    high = lax.reduce_precision(x, 8, 7)
    return high.astype(bf16), (x - high).astype(bf16)


def map_parts(matrix):
    high, low = two_parts(matrix)
    return jnp.concatenate([high, low, high], axis=1)


def state_parts(x):
    high = x.astype(bf16)
    low = (x - high.astype(f32)).astype(bf16)
    return jnp.concatenate([high, high, low], axis=0)


def dot32(a, b):
    return jnp.dot(a, b, preferred_element_type=f32)


def local_kernel(
    blocks, per, noise, gauges, weights, spread, retain, keep, fwd_map, bwd_map, trans,
    partial, maps, end_state, end_map, first_state, first_map,
    filt, filt_x, pred, pred_x, run, run_x,
):
    step = pl.program_id(0)
    width = trans.shape[0]

    @pl.when(step == 0)
    def _():
        run[...] = jnp.zeros_like(run)
        run_x[...] = jnp.concatenate([trans[...], jnp.zeros_like(trans)], axis=1)

    @pl.when(step < blocks)
    def _():
        p, px = run[...], run_x[...]
        for i in range(per):
            t = step * per + i
            scaled = (spread[...] * noise[i].astype(f32)).astype(bf16)
            reads = gauges[i]
            offset = dot32(weights[i], jnp.concatenate([scaled, reads, reads], axis=0))
            rate = retain[t]
            f = rate * p + offset
            fx = rate * px
            filt[t] = f
            filt_x[t] = fx
            p = dot32(fwd_map[...], state_parts(f))
            px = dot32(fwd_map[...], state_parts(fx))
            pred[t] = p
            pred_x[t] = px
        run[...] = p
        run_x[...] = px

        @pl.when(step == blocks - 1)
        def _():
            end_state[...] = f
            end_map[...] = fx
            run[...] = jnp.zeros_like(run)
            row = lax.broadcasted_iota(jnp.int32, run_x.shape, 0)
            col = lax.broadcasted_iota(jnp.int32, run_x.shape, 1)
            run_x[...] = jnp.where(col == row + width, 1.0, 0.0)

    @pl.when(step >= blocks)
    def _():
        s, sx = run[...], run_x[...]
        for i in reversed(range(per)):
            t = (2 * blocks - 1 - step) * per + i
            rate = keep[t]
            s = filt[t] + dot32(bwd_map[...], state_parts(rate * (s - pred[t])))
            sx = filt_x[t] + dot32(bwd_map[...], state_parts(rate * (sx - pred_x[t])))
            partial[i] = s
            maps[i] = sx
        run[...] = s
        run_x[...] = sx

        @pl.when(step == 2 * blocks - 1)
        def _():
            first_state[...] = s
            first_map[...] = sx


def local_pass(noise, gauges, weights, spread, retain, keep, fwd_map, bwd_map, trans):
    steps, width, runs = noise.shape
    per = 4
    blocks = steps // per
    ahead = lambda i: (jnp.minimum(i, blocks - 1), 0, 0)
    back = lambda i: (jnp.minimum(2 * blocks - 1 - i, blocks - 1), 0, 0)
    whole2 = lambda i: (0, 0)
    whole3 = lambda i: (0, 0, 0)
    full = lambda x: pl.BlockSpec(x.shape, whole3 if x.ndim == 3 else whole2)
    extra = 2 * width
    body = lambda *refs: local_kernel(blocks, per, *refs)
    return pl.pallas_call(
        body,
        grid=(2 * blocks,),
        in_specs=[
            pl.BlockSpec((per,) + noise.shape[1:], ahead),
            pl.BlockSpec((per,) + gauges.shape[1:], ahead),
            pl.BlockSpec((per,) + weights.shape[1:], ahead),
            full(spread), full(retain), full(keep), full(fwd_map), full(bwd_map), full(trans),
        ],
        out_specs=[
            pl.BlockSpec((per, width, runs), back),
            pl.BlockSpec((per, width, extra), back),
            pl.BlockSpec((width, runs), whole2),
            pl.BlockSpec((width, extra), whole2),
            pl.BlockSpec((width, runs), whole2),
            pl.BlockSpec((width, extra), whole2),
        ],
        out_shape=[
            jax.ShapeDtypeStruct((steps, width, runs), f32),
            jax.ShapeDtypeStruct((steps, width, extra), f32),
            jax.ShapeDtypeStruct((width, runs), f32),
            jax.ShapeDtypeStruct((width, extra), f32),
            jax.ShapeDtypeStruct((width, runs), f32),
            jax.ShapeDtypeStruct((width, extra), f32),
        ],
        scratch_shapes=[
            pltpu.VMEM((steps, width, runs), f32),
            pltpu.VMEM((steps, width, extra), f32),
            pltpu.VMEM((steps, width, runs), f32),
            pltpu.VMEM((steps, width, extra), f32),
            pltpu.VMEM((width, runs), f32),
            pltpu.VMEM((width, extra), f32),
        ],
        compiler_params=pltpu.CompilerParams(vmem_limit_bytes=52 * 2**20),
    )(noise, gauges, weights, spread, retain, keep, fwd_map, bwd_map, trans)


def split_dot(matrix, state):
    high = matrix.astype(bf16)
    low = (matrix - high.astype(f32)).astype(bf16)
    return dot32(jnp.concatenate([high, low, high], axis=1), state_parts(state))


def border_kernel(states, maps, carries):
    count, double, runs = states.shape
    width = double // 2
    carry = jnp.zeros((width, runs), f32)
    for d in range(count):
        carries[d, :width] = carry
        if d < count - 1:
            carry = states[d, :width] + split_dot(maps[d, :, : 2 * width], jnp.concatenate([carry, jnp.zeros_like(carry)], axis=0))
    carry = jnp.zeros((width, runs), f32)
    for d in reversed(range(count)):
        carries[d, width:] = carry
        if d > 0:
            carry = states[d, width:] + split_dot(
                maps[d, :, 2 * width :], jnp.concatenate([carries[d, :width], carry], axis=0)
            )


def border_pass(states, maps):
    return pl.pallas_call(
        border_kernel,
        out_shape=jax.ShapeDtypeStruct(states.shape, f32),
        compiler_params=pltpu.CompilerParams(vmem_limit_bytes=32 * 2**20),
    )(states, maps)


def close_kernel(per, partial, maps, carries, smoothed, parts):
    @pl.when(pl.program_id(0) == 0)
    def _():
        parts[...] = state_parts(carries[...])

    for i in range(per):
        m = maps[i]
        high = m.astype(bf16)
        low = (m - high.astype(f32)).astype(bf16)
        smoothed[i] = partial[i] + dot32(jnp.concatenate([high, low, high], axis=1), parts[...])


def close_pass(partial, maps, carries):
    steps, width, runs = partial.shape
    per = 4
    body = lambda *refs: close_kernel(per, *refs)
    along = lambda i: (i, 0, 0)
    return pl.pallas_call(
        body,
        grid=(steps // per,),
        in_specs=[
            pl.BlockSpec((per, width, runs), along),
            pl.BlockSpec((per,) + maps.shape[1:], along),
            pl.BlockSpec(carries.shape, lambda i: (0, 0)),
        ],
        out_specs=pl.BlockSpec((per, width, runs), along),
        out_shape=jax.ShapeDtypeStruct(partial.shape, f32),
        scratch_shapes=[pltpu.VMEM((3 * carries.shape[0], runs), bf16)],
        compiler_params=pltpu.CompilerParams(vmem_limit_bytes=32 * 2**20),
    )(partial, maps, carries)


def shards(
    process_noise,
    gauge_reads,
    sensor_active,
    sensor_link,
    reflectors,
    decay_rates,
    turn_angles,
    gauge_gain,
):
    steps, width, runs = process_noise.shape
    count = lax.axis_size("tm")
    rotation = rotation_basis(reflectors)
    blocks = pair_blocks(decay_rates, turn_angles)
    transition = jnp.dot(
        jnp.dot(rotation, blocks, precision=exact_mode), rotation.T, precision=exact_mode
    )
    positions = jnp.arange(width)
    onehot = (positions[None, :] == 2 * sensor_link[:, None]).astype(f32)
    active = sensor_active.astype(f32)
    counts = jnp.dot(active, onehot, precision=exact_mode)
    retain = jnp.exp(counts * jnp.log1p(-gauge_gain)[None, :])
    spread = jnp.repeat(jnp.sqrt(-jnp.expm1(-2.0 * decay_rates)), 2)
    last_row = (jnp.arange(steps) == steps - 1)[:, None]
    final_device = lax.axis_index("tm") == count - 1
    keep = jnp.where(jnp.logical_and(last_row, final_device), 0.0, retain)
    gain_high, gain_low = two_parts(gauge_gain)
    placed = (onehot.T.astype(bf16))[None] * sensor_active.astype(bf16)[:, None, :]
    weights = jnp.concatenate(
        [
            jnp.broadcast_to(rotation.astype(bf16)[None], (steps, width, width)),
            gain_high[None, :, None] * placed,
            gain_low[None, :, None] * placed,
        ],
        axis=2,
    )
    partial, maps, end_state, end_map, first_state, first_map = local_pass(
        process_noise, gauge_reads, weights, spread[:, None], retain[:, :, None],
        keep[:, :, None], map_parts(transition), map_parts(transition.T), transition,
    )
    own = jnp.concatenate([end_state, first_state], axis=0)
    own = own.reshape(2 * width, count, runs // count).transpose(1, 0, 2)
    states = lax.all_to_all(own, "tm", 0, 0)
    all_maps = lax.all_gather(jnp.concatenate([end_map, first_map], axis=1), "tm")
    carries = border_pass(states, all_maps)
    carries = lax.all_to_all(carries, "tm", 0, 0)
    carries = carries.transpose(1, 0, 2).reshape(2 * width, runs)
    return close_pass(partial, maps, carries)


def solution(mesh):
    in_specs = (
        P(("groups", "tm"), None, None),
        P(("groups", "tm"), None, None),
        P(("groups", "tm"), None),
        P(),
        P("groups", None),
        P("groups"),
        P("groups"),
        P("groups"),
    )
    out_specs = P(("groups", "tm"), None, None)
    return jax.shard_map(shards, mesh=mesh, in_specs=in_specs, out_specs=out_specs, check_vma=False)
```

profile of v0, /device:TPU:0, one launch (start us, length us, event | category | flops | bytes accessed | tf_op | source)
XLA Modules:
  0.0 131.0 jit_solution(7283716013141832499)
XLA Ops:
  6.5 0.8 convolution_bitcast_fusion.3
  7.3 1.5 %multiply_reduce_fusion = (f32[]{:T(128)}, f32[]{:T(128)}, f32[]{:T(128)}, f32[]{:T(128)}) fusion(f32[4,64]{1,0:T(4,128)} %param.12), kind=kLoop, calls=%fused_computation.81 | loop fusion | flops 508 | bytes 1040 | tf_op jit(solution)/shard_map/reduce_sum | solution.py:18
  8.9 0.8 slice_bitcast_fusion.3
  9.7 0.7 broadcast_multiply_fusion
  10.4 0.7 negate_log-plus-one_fusion
  13.7 0.7 convert_element_type.58
  14.5 0.9 fusion
  15.4 0.7 cosine_multiply_fusion
  16.6 0.9 convolution_bitcast_fusion.2
  17.5 0.9 convolution_bitcast_fusion.1
  18.5 0.9 convolution_bitcast_fusion
  20.3 1.4 %copy.31.refs_5_ = f32[32,64,1]{2,1,0:T(8,128)} copy(f32[32,64,1]{1,0,2:T(8,128)S(1)} %fusion.9) | data formatting | bytes 16384 | tf_op jit(solution)/shard_map/broadcast_in_dim | solution.py:271
  21.7 1.4 %copy.30.refs_4_ = f32[32,64,1]{2,1,0:T(8,128)} copy(f32[32,64,1]{1,0,2:T(8,128)S(1)} %bitcast.58) | data formatting | bytes 16384 | tf_op jit(solution)/shard_map/broadcast_in_dim | solution.py:270
  23.6 1.6 %pad_maximum_fusion.refs_2_ = bf16[32,64,256]{2,1,0:T(8,128)(2,1)} fusion(bf16[32,64,96]{2,1,0:T(8,128)(2,1)S(1)} %get-tuple-element.26, bf16[32,64,96]{2,1,0:T(8,128)(2,1)S(1)} %get-tuple-element.25, bf16[32,64,64]{2,1,0:T(8,128)(2,1)S(1)} %broadcast_in_dim.46), kind=kLoop, calls=%fused_computation.6 | loop fusion | flops 3145728 | bytes 2097152 | tf_op jit(solution)/shard_map/concatenate | solution.py:261
  25.2 20.7 %shard_map.82 = (f32[32,64,1024]{2,1,0:T(8,128)}, f32[32,64,128]{2,1,0:T(8,128)S(1)}, f32[64,1024]{1,0:T(8,128)S(1)}, f32[64,128]{1,0:T(8,128)S(1)}, f32[64,1024]{1,0:T(8,128)S(1)}, /*index=5*/f32[64,128]{1,0:T(8,128)S(1)}) custom-call(bf16[32,64,1024]{2,1,0:T(8,128)(2,1)} %refs_0_.1, bf16[32,96,1024]{2,1,0:T(8,128)(2,1)} %refs_1_.1, ...), custom_call_target="tpu_custom_call" | custom-call | tf_op jit(solution)/shard_map/pallas_call | solution.py:133
  45.9 0.6 pad_maximum_fusion.2
  46.8 23.1 %all_to_all.10 = f32[16,128,64]{1,2,0:T(8,128)S(1)} all-to-all(f32[16,128,64]{1,2,0:T(8,128)S(1)} %bitcast.56), channel_id=1, replica_groups=mesh['groups'=2,'tm'=16] {'tm'}, dimensions={0} | all-to-all | bytes 1048576 | tf_op jit(solution)/shard_map/all_to_all | solution.py:275
  69.8 0.3 copy.33.states
  70.2 19.2 %all-gather.3.cloned.1.call-done = f32[1024,256]{1,0:T(8,128)} async-done(((f32[64,256]{1,0:T(8,128)}), f32[1024,256]{1,0:T(8,128)}) %all-gather.3.cloned.1.call-update) | async-done | bytes 1048592 | tf_op jit(solution)/shard_map/all_gather | solution.py:276
  89.4 1.2 copy-done.1
  90.6 4.3 %shard_map.83 = f32[16,128,64]{2,1,0:T(8,128)S(1)} custom-call(f32[16,128,64]{2,1,0:T(8,128)S(1)} %copy.33.states, f32[16,64,256]{2,1,0:T(8,128)S(1)} %bitcast.55), custom_call_target="tpu_custom_call" | custom-call | tf_op jit(solution)/shard_map/pallas_call | solution.py:194
  95.2 17.9 %all_to_all.11 = f32[16,128,64]{1,2,0:T(8,128)S(1)} all-to-all(f32[16,128,64]{1,2,0:T(8,128)S(1)} %copy.34), channel_id=1, replica_groups=mesh['groups'=2,'tm'=16] {'tm'}, dimensions={0} | all-to-all | bytes 1048576 | tf_op jit(solution)/shard_map/all_to_all | solution.py:278
  113.4 3.4 %copy-done = f32[32,64,1024]{2,1,0:T(8,128)S(1)} copy-done((f32[32,64,1024]{2,1,0:T(8,128)S(1)}, f32[32,64,1024]{2,1,0:T(8,128)}, u32[]{:S(2)}) %copy-start) | copy-done | bytes 8388632
  116.7 7.4 %shard_map.84 = f32[32,64,1024]{2,1,0:T(8,128)} custom-call(f32[32,64,1024]{2,1,0:T(8,128)S(1)} %copy-done, f32[32,64,128]{2,1,0:T(8,128)S(1)} %get-tuple-element.12.refs_1_, f32[128,1024]{1,0:T(8,128)S(1)} %copy.35.refs_2_), custom_call_target="tpu_custom_call" | custom-call | tf_op jit(solution)/shard_map/pallas_call | solution.py:218
  (28 shorter events, 2.6 us)
Async XLA Ops:
  6.5 82.9 %all-gather.3.cloned.1.call-start = ((), (), s32[]{:S(2)}) async-start(), calls=%async_computation.2 | async-start | bytes 1114112 | tf_op jit(solution)/shard_map/all_gather | solution.py:276
  89.4 1.2 copy-start.1
  113.3 3.4 %copy-start = (f32[32,64,1024]{2,1,0:T(8,128)S(1)}, f32[32,64,1024]{2,1,0:T(8,128)}, u32[]{:S(2)}) copy-start(f32[32,64,1024]{2,1,0:T(8,128)} %get-tuple-element.11.refs_0_) | copy-start | bytes 25165828
Sparse Core Ops, SparseCore 0:
  46.7 42.6 all-gather.2
where the time goes:
time: 132 us; the launch traced here: 131 us
  blocking collectives  41 us (31%)
  Pallas kernels  32.4 us (25%)
  waiting for transfers between devices  19.2 us (15%)
  between operations  16.2 us (12%)
  local copies, waits for them, and re-layouts  10 us (8%)
  other arithmetic  7.12 us (5%)
  matrix products  5.06 us (4%)
    all_to_all x1, blocking collectives, shards(): states = lax.all_to_all(own, 'tm', 0, 0)  23.1 us
    pallas_call x1, Pallas kernels, local_pass(): pl.pallas_call(body, grid=(2 * blocks,), in_specs=[pl.BlockSpec((per,) +...  20.7 us
    all_gather x1, waiting for transfers between devices, shards(): lax.all_gather(jnp.concatenate([end_map, first_map], axis=1), 'tm')  19.2 us
    all_to_all x1, blocking collectives, shards(): carries = lax.all_to_all(carries, 'tm', 0, 0)  17.9 us
    pallas_call x1, Pallas kernels, close_pass(): pl.pallas_call(body, grid=(steps // per,), in_specs=[pl.BlockSpec((per, w...  7.39 us
    unnamed x4, local copies, waits for them, and re-layouts  4.6 us
    pallas_call x1, Pallas kernels, border_pass(): pl.pallas_call(border_kernel, out_shape=jax.ShapeDtypeStruct(states.shape...  4.29 us
    dot_general x4, matrix products, rotation_basis(): jnp.dot(rotation, vector, precision=exact_mode)  3.56 us
  transfers between devices with their start and end apart: 1, of which 1 were waited for; matrix products, arithmetic and copies ran while one was open for 0% of the time, Pallas kernels for 0%

commit v1 on v0

--- a/solution.py
+++ b/solution.py
@@ -173,29 +173,103 @@
     return dot32(jnp.concatenate([high, low, high], axis=1), state_parts(state))
 
 
-def border_kernel(states, maps, carries):
-    count, double, runs = states.shape
-    width = double // 2
+def border_kernel(
+    count, group, own, own_map, result, states, maps, carries, landed,
+    state_send, state_recv, far_send, far_recv, near_send, near_recv, back_send, back_recv,
+):
+    me = lax.axis_index("tm")
+    width, double = own.shape[1:]
+    runs = double // 2
+    far = count // group
+    place, seat = lax.div(me, group), lax.rem(me, group)
+
+    def push(source, target, send, recv, where):
+        copy = pltpu.make_async_remote_copy(
+            src_ref=source, dst_ref=target, send_sem=send, recv_sem=recv,
+            device_id={"tm": where}, device_id_type=pl.DeviceIdType.MESH,
+        )
+        copy.start()
+        return copy
+
+    barrier = pltpu.get_barrier_semaphore()
+    for k in range(1, count):
+        pl.semaphore_signal(
+            barrier, inc=1, device_id={"tm": lax.rem(me + k, count)},
+            device_id_type=pl.DeviceIdType.MESH,
+        )
+    pl.semaphore_wait(barrier, count - 1)
+
+    far_copies = [
+        push(own_map, maps.at[seat, place], far_send.at[k], far_recv.at[k],
+             lax.rem(place + k, far) * group + seat)
+        for k in range(1, far)
+    ]
+    copies = [
+        push(own.at[lax.rem(me + k, count)], states.at[me], state_send.at[k], state_recv.at[k],
+             lax.rem(me + k, count))
+        for k in range(1, count)
+    ]
+    states[me] = own[me]
+    maps[seat, place] = own_map[...]
+    for copy in far_copies:
+        copy.wait()
+    copies += [
+        push(maps.at[seat], maps.at[seat], near_send.at[k], near_recv.at[k],
+             place * group + lax.rem(seat + k, group))
+        for k in range(1, group)
+    ]
+    for copy in copies:
+        copy.wait()
+
     carry = jnp.zeros((width, runs), f32)
+    ahead, pulled = [], []
     for d in range(count):
-        carries[d, :width] = carry
+        both = maps[d % group, d // group]
+        stay, turn = both[:, :width], both[:, width:]
+        ahead.append(carry)
+        pulled.append(states[d, :, runs:] + split_dot(turn, carry))
         if d < count - 1:
-            carry = states[d, :width] + split_dot(maps[d, :, : 2 * width], jnp.concatenate([carry, jnp.zeros_like(carry)], axis=0))
+            carry = states[d, :, :runs] + split_dot(stay, carry)
     carry = jnp.zeros((width, runs), f32)
     for d in reversed(range(count)):
-        carries[d, width:] = carry
+        carries[d] = jnp.concatenate([ahead[d], carry], axis=1)
         if d > 0:
-            carry = states[d, width:] + split_dot(
-                maps[d, :, 2 * width :], jnp.concatenate([carries[d, :width], carry], axis=0)
-            )
-
-
-def border_pass(states, maps):
+            stay = maps[d % group, d // group][:, :width]
+            carry = pulled[d] + split_dot(stay.T, carry)
+
+    copies = [
+        push(carries.at[lax.rem(me + k, count)], landed.at[me], back_send.at[k], back_recv.at[k],
+             lax.rem(me + k, count))
+        for k in range(1, count)
+    ]
+    landed[me] = carries[me]
+    for copy in copies:
+        copy.wait()
+    result[...] = landed[...]
+
+
+def border_pass(own, own_map):
+    count = own.shape[0]
+    group = 4 if count % 4 == 0 else 1
+    far = count // group
+    dma = pltpu.SemaphoreType.DMA
     return pl.pallas_call(
-        border_kernel,
-        out_shape=jax.ShapeDtypeStruct(states.shape, f32),
-        compiler_params=pltpu.CompilerParams(vmem_limit_bytes=32 * 2**20),
-    )(states, maps)
+        lambda *refs: border_kernel(count, group, *refs),
+        in_specs=[pl.BlockSpec(memory_space=pltpu.VMEM)] * 2,
+        out_specs=pl.BlockSpec(memory_space=pltpu.VMEM),
+        out_shape=jax.ShapeDtypeStruct(own.shape, f32),
+        scratch_shapes=[
+            pltpu.VMEM(own.shape, f32),
+            pltpu.VMEM((group, far) + own_map.shape, f32),
+            pltpu.VMEM(own.shape, f32),
+            pltpu.VMEM(own.shape, f32),
+            dma((count,)), dma((count,)), dma((far,)), dma((far,)),
+            dma((group,)), dma((group,)), dma((count,)), dma((count,)),
+        ],
+        compiler_params=pltpu.CompilerParams(
+            collective_id=0, has_side_effects=True, vmem_limit_bytes=32 * 2**20
+        ),
+    )(own, own_map)
 
 
 def close_kernel(per, partial, maps, carries, smoothed, parts):
@@ -270,13 +344,12 @@
         process_noise, gauge_reads, weights, spread[:, None], retain[:, :, None],
         keep[:, :, None], map_parts(transition), map_parts(transition.T), transition,
     )
-    own = jnp.concatenate([end_state, first_state], axis=0)
-    own = own.reshape(2 * width, count, runs // count).transpose(1, 0, 2)
-    states = lax.all_to_all(own, "tm", 0, 0)
-    all_maps = lax.all_gather(jnp.concatenate([end_map, first_map], axis=1), "tm")
-    carries = border_pass(states, all_maps)
-    carries = lax.all_to_all(carries, "tm", 0, 0)
-    carries = carries.transpose(1, 0, 2).reshape(2 * width, runs)
+    sliced = lambda x: x.reshape(width, count, runs // count).transpose(1, 0, 2)
+    own = jnp.concatenate([sliced(end_state), sliced(first_state)], axis=2)
+    own_map = jnp.concatenate([end_map[:, :width], first_map[:, :width]], axis=1)
+    carries = border_pass(own, own_map)
+    carries = carries.reshape(count, width, 2, runs // count).transpose(2, 1, 0, 3)
+    carries = carries.reshape(2 * width, runs)
     return close_pass(partial, maps, carries)
 
 

time: 132 us -> 94 us (0.71)
  blocking collectives: 41 us -> 0 us
  Pallas kernels: 32.4 us -> 67.7 us
  waiting for transfers between devices: 19.2 us -> 0 us
  between operations: 16.2 us -> 2.84 us
    all_to_all x2 -> x0, blocking collectives: 41 us -> none  [the longest x1 23.1 us: shards(): states = lax.all_to_all(own, 'tm', 0, 0)]
    pallas_call x1, Pallas kernels: 4.29 us -> 39.6 us  [border_pass(): pl.pallas_call(lambda *refs: border_kernel(count, group, *refs), in_specs...]
    all_gather x1 -> x0, waiting for transfers between devices: 19.2 us -> none  [shards(): lax.all_gather(jnp.concatenate([end_map, first_map], axis=1), 'tm')]
    reshape x1 -> x7, local copies, waits for them, and re-layouts: 0.2 us -> 2.15 us  [the longest x2 1.22 us: shards(): carries.reshape(count, width, 2, runs // count).transpose(2, 1, 0, 3)]
    unnamed x4 -> x2, local copies, waits for them, and re-layouts: 4.6 us -> 3.38 us
  transfers between devices with their start and end apart: 1 -> 0, of which waited for: 1 -> 0; matrix products, arithmetic and copies ran while one was open for 0% -> 0% of each run, Pallas kernels for 0% -> 0%
where the time goes in v1:
time: 94 us; the launch traced here: 92.3 us
  Pallas kernels  67.7 us (72%)
  local copies, waits for them, and re-layouts  9.88 us (11%)
  other arithmetic  6.8 us (7%)
  matrix products  5.05 us (5%)
  between operations  2.84 us (3%)
    pallas_call x1, Pallas kernels, border_pass(): pl.pallas_call(lambda *refs: border_kernel(count, group, *refs), in_specs...  39.6 us
    pallas_call x1, Pallas kernels, local_pass(): pl.pallas_call(body, grid=(2 * blocks,), in_specs=[pl.BlockSpec((per,) +...  20.7 us
    pallas_call x1, Pallas kernels, close_pass(): pl.pallas_call(body, grid=(steps // per,), in_specs=[pl.BlockSpec((per, w...  7.39 us
    dot_general x4, matrix products, rotation_basis(): jnp.dot(rotation, vector, precision=exact_mode)  3.55 us
    unnamed x2, local copies, waits for them, and re-layouts  3.38 us

profile of v1, /device:TPU:0, one launch (start us, length us, event | category | flops | bytes accessed | tf_op | source)
XLA Modules:
  0.0 92.3 jit_solution(17938865965071201112)
XLA Ops:
  0.0 0.8 convolution_bitcast_fusion.3
  0.8 0.7 broadcast_multiply_fusion
  1.5 0.7 cosine_multiply_fusion
  2.2 0.7 negate_log-plus-one_fusion
  2.9 1.5 %multiply_reduce_fusion = (f32[]{:T(128)}, f32[]{:T(128)}, f32[]{:T(128)}, f32[]{:T(128)}) fusion(f32[4,64]{1,0:T(4,128)} %param.12), kind=kLoop, calls=%fused_computation.84 | loop fusion | flops 508 | bytes 1040 | tf_op jit(solution)/shard_map/reduce_sum | solution.py:18
  7.1 0.8 slice_bitcast_fusion.3
  7.9 0.9 convolution_bitcast_fusion.2
  8.8 0.9 %convolution_bitcast_fusion.1 = f32[64]{0:T(128)S(1)} fusion(f32[64]{0:T(128)S(1)} %get-tuple-element.28, f32[64]{0:T(128)S(1)} %convolution_bitcast_fusion.2, f32[]{:T(128)S(6)} %div.19, f32[64]{0:T(128)S(1)} %get-tuple-element.27, f32[64]{0:T(128)S(1)} %convolution_bitcast_fusion.3, f32[]{:T(128)S(6)} %div.18, f32[4,64]{1,0:T(4,128)} %param.12), kind=kOutput, calls=%fused_computation.3 | convolution fusion | flops 81920 | bytes 1800 | tf_op jit(solution)/shard_map/dot_general | solution.py:20
  9.8 0.9 %convolution_bitcast_fusion = f32[64]{0:T(128)S(1)} fusion(f32[64]{0:T(128)S(1)} %get-tuple-element.30, f32[64]{0:T(128)S(1)} %convolution_bitcast_fusion.1, f32[]{:T(128)S(6)} %div.20, f32[64]{0:T(128)S(1)} %get-tuple-element.28, f32[64]{0:T(128)S(1)} %convolution_bitcast_fusion.2, f32[]{:T(128)S(6)} %div.19, f32[64]{0:T(128)S(1)} %get-tuple-element.27, ...), kind=kOutput, calls=%fused_computation.2 | convolution fusion | flops 94208 | bytes 2316 | tf_op jit(solution)/shard_map/dot_general | solution.py:20
  10.7 0.8 convert_element_type.58
  11.5 0.9 %fusion = f32[64,32]{0,1:T(8,128)S(1)} fusion(s32[96]{0:T(128)S(1)} %broadcast_multiply_fusion, s32[32,96]{1,0:T(8,128)} %param.10, f32[64]{0:T(128)S(1)} %get-tuple-element.34), kind=kOutput, calls=%fused_computation.1 | convolution fusion | flops 2370560 | bytes 21120 | tf_op jit(solution)/shard_map/dot_general | solution.py:327
  13.1 0.3 fusion.3
  13.4 0.3 fusion.1
  14.2 1.6 %pad_maximum_fusion.refs_2_ = bf16[32,64,256]{2,1,0:T(8,128)(2,1)} fusion(bf16[32,64,96]{2,1,0:T(8,128)(2,1)S(1)} %get-tuple-element.26, bf16[32,64,96]{2,1,0:T(8,128)(2,1)S(1)} %get-tuple-element.25, bf16[32,64,64]{2,1,0:T(8,128)(2,1)S(1)} %broadcast_in_dim.46), kind=kLoop, calls=%fused_computation.6 | loop fusion | flops 3145728 | bytes 2097152 | tf_op jit(solution)/shard_map/concatenate | solution.py:335
  15.9 1.4 %copy.22.refs_5_ = f32[32,64,1]{2,1,0:T(8,128)} copy(f32[32,64,1]{1,0,2:T(8,128)S(1)} %fusion.9) | data formatting | bytes 16384 | tf_op jit(solution)/shard_map/broadcast_in_dim | solution.py:345
  17.3 1.4 %copy.21.refs_4_ = f32[32,64,1]{2,1,0:T(8,128)} copy(f32[32,64,1]{1,0,2:T(8,128)S(1)} %bitcast.66) | data formatting | bytes 16384 | tf_op jit(solution)/shard_map/broadcast_in_dim | solution.py:344
  18.7 20.7 %shard_map.82 = (f32[32,64,1024]{2,1,0:T(8,128)}, f32[32,64,128]{2,1,0:T(8,128)S(1)}, f32[64,1024]{1,0:T(8,128)S(1)}, f32[64,128]{1,0:T(8,128)S(1)}, f32[64,1024]{1,0:T(8,128)S(1)}, /*index=5*/f32[64,128]{1,0:T(8,128)S(1)}) custom-call(bf16[32,64,1024]{2,1,0:T(8,128)(2,1)} %refs_0_.1, bf16[32,96,1024]{2,1,0:T(8,128)(2,1)} %refs_1_.1, ...), custom_call_target="tpu_custom_call" | custom-call | tf_op jit(solution)/shard_map/pallas_call | solution.py:133
  40.1 0.2 pad_maximum_fusion.1.refs_0_
  40.3 39.6 %shard_map.83 = f32[16,64,128]{2,1,0:T(8,128)S(1)} custom-call(f32[16,64,128]{2,1,0:T(8,128)S(1)} %pad_maximum_fusion.1.refs_0_, f32[64,128]{1,0:T(8,128)S(1)} %pad_maximum_fusion.4.refs_1_), custom_call_target="tpu_custom_call" | custom-call | tf_op jit(solution)/shard_map/pallas_call | solution.py:256
  79.9 0.6 reshape.240
  80.5 0.6 copy.29
  81.2 0.3 reshape.241.refs_2_
  81.5 3.4 %copy-done = f32[32,64,1024]{2,1,0:T(8,128)S(1)} copy-done((f32[32,64,1024]{2,1,0:T(8,128)S(1)}, f32[32,64,1024]{2,1,0:T(8,128)}, u32[]{:S(2)}) %copy-start) | copy-done | bytes 8388632
  84.9 7.4 %shard_map.84 = f32[32,64,1024]{2,1,0:T(8,128)} custom-call(f32[32,64,1024]{2,1,0:T(8,128)S(1)} %copy-done, f32[32,64,128]{2,1,0:T(8,128)S(1)} %get-tuple-element.12.refs_1_, f32[128,1024]{1,0:T(8,128)S(1)} %reshape.241.refs_2_), custom_call_target="tpu_custom_call" | custom-call | tf_op jit(solution)/shard_map/pallas_call | solution.py:292
  (24 shorter events, 1.9 us)
Async XLA Ops:
  81.5 3.4 %copy-start = (f32[32,64,1024]{2,1,0:T(8,128)S(1)}, f32[32,64,1024]{2,1,0:T(8,128)}, u32[]{:S(2)}) copy-start(f32[32,64,1024]{2,1,0:T(8,128)} %get-tuple-element.11.refs_0_) | copy-start | bytes 25165828

commit v2 on v0

--- a/solution.py
+++ b/solution.py
@@ -173,29 +173,134 @@
     return dot32(jnp.concatenate([high, low, high], axis=1), state_parts(state))
 
 
-def border_kernel(states, maps, carries):
-    count, double, runs = states.shape
-    width = double // 2
-    carry = jnp.zeros((width, runs), f32)
-    for d in range(count):
-        carries[d, :width] = carry
-        if d < count - 1:
-            carry = states[d, :width] + split_dot(maps[d, :, : 2 * width], jnp.concatenate([carry, jnp.zeros_like(carry)], axis=0))
-    carry = jnp.zeros((width, runs), f32)
-    for d in reversed(range(count)):
-        carries[d, width:] = carry
-        if d > 0:
-            carry = states[d, width:] + split_dot(
-                maps[d, :, 2 * width :], jnp.concatenate([carries[d, :width], carry], axis=0)
+def border_kernel(sizes, end_state, first_state, end_map, first_map, result, *scratch):
+    me = lax.axis_index("tm")
+    width = end_state.shape[0]
+    last = len(sizes) - 1
+    strides, seats = [], []
+    stride = 1
+    for size in sizes:
+        strides.append(stride)
+        seats.append(lax.rem(lax.div(me, stride), size))
+        stride *= size
+
+    def peer(level, k):
+        seat = seats[level]
+        return me + (lax.rem(seat + k, sizes[level]) - seat) * strides[level]
+
+    barrier = pltpu.get_barrier_semaphore()
+    for level, size in enumerate(sizes):
+        for k in range(1, size):
+            pl.semaphore_signal(
+                barrier, inc=1, device_id={"tm": peer(level, k)},
+                device_id_type=pl.DeviceIdType.MESH,
             )
-
-
-def border_pass(states, maps):
+    pl.semaphore_wait(barrier, sum(sizes) - len(sizes))
+
+    def push(source, target, send, recv, where):
+        copy = pltpu.make_async_remote_copy(
+            src_ref=source, dst_ref=target, send_sem=send, recv_sem=recv,
+            device_id={"tm": where}, device_id_type=pl.DeviceIdType.MESH,
+        )
+        copy.start()
+        return copy
+
+    def solve(level, state, first, stay, turn):
+        own, got, maps, back, landed, *sems = scratch[11 * level : 11 * (level + 1)]
+        size, seat = sizes[level], seats[level]
+        runs = state.shape[1] // size
+        top = level == last
+        maps[seat] = jnp.concatenate([stay, turn], axis=1)
+        for j in range(size):
+            part = slice(j * runs, (j + 1) * runs)
+            own[j] = jnp.concatenate([state[:, part], first[:, part]], axis=1)
+        copies = []
+        for k in range(1, size):
+            where = peer(level, k)
+            copies.append(push(maps.at[seat], maps.at[seat], sems[0].at[k], sems[1].at[k], where))
+            copies.append(
+                push(own.at[lax.rem(seat + k, size)], got.at[seat], sems[2].at[k], sems[3].at[k], where)
+            )
+        got[seat] = own[seat]
+        for copy in copies:
+            copy.wait()
+
+        row = lax.broadcasted_iota(jnp.int32, (width, 2 * width), 0)
+        col = lax.broadcasted_iota(jnp.int32, (width, 2 * width), 1)
+        zero = jnp.zeros((width, runs), f32)
+        blank = jnp.zeros((width, 2 * width), f32)
+
+        def wide(value, extra):
+            return value if top else jnp.concatenate([value, extra], axis=1)
+
+        ahead, pulled, behind = [], [], [None] * size
+        carry = wide(zero, jnp.where(row == col, 1.0, 0.0))
+        for d in range(size):
+            tile, both = got[d], maps[d]
+            ahead.append(carry)
+            pulled.append(wide(tile[:, runs:], blank) + split_dot(both[:, width:], carry))
+            if not (top and d == size - 1):
+                carry = wide(tile[:, :runs], blank) + split_dot(both[:, :width], carry)
+        end = carry
+        carry = wide(zero, jnp.where(row + width == col, 1.0, 0.0))
+        for d in reversed(range(size)):
+            behind[d] = carry
+            if not (top and d == 0):
+                carry = pulled[d] + split_dot(maps[d][:, :width].T, carry)
+        if not top:
+            inner = slice(runs, runs + width)
+            outer = jnp.concatenate(
+                solve(level + 1, end[:, :runs], carry[:, :runs], end[:, inner], carry[:, inner]),
+                axis=0,
+            )
+        for d in range(size):
+            f, s = ahead[d], behind[d]
+            if not top:
+                f = f[:, :runs] + split_dot(f[:, runs:], outer)
+                s = s[:, :runs] + split_dot(s[:, runs:], outer)
+            back[d] = jnp.concatenate([f, s], axis=1)
+        copies = [
+            push(back.at[lax.rem(seat + k, size)], landed.at[seat], sems[4].at[k], sems[5].at[k],
+                 peer(level, k))
+            for k in range(1, size)
+        ]
+        landed[seat] = back[seat]
+        for copy in copies:
+            copy.wait()
+        tiles = [landed[j] for j in range(size)]
+        return (
+            jnp.concatenate([t[:, :runs] for t in tiles], axis=1),
+            jnp.concatenate([t[:, runs:] for t in tiles], axis=1),
+        )
+
+    incoming, later = solve(
+        0, end_state[...], first_state[...], end_map[:, :width], first_map[:, :width]
+    )
+    result[:width] = incoming
+    result[width:] = later
+
+
+def border_pass(end_state, first_state, end_map, first_map):
+    count = lax.axis_size("tm")
+    width, runs = end_state.shape
+    sizes = (2, 2, count // 4) if count % 4 == 0 and count > 4 else (count,)
+    scratch = []
+    piece = runs
+    for size in sizes:
+        piece //= size
+        tiles = pltpu.VMEM((size, width, 2 * piece), f32)
+        scratch += [tiles, tiles, pltpu.VMEM((size, width, 2 * width), f32), tiles, tiles]
+        scratch += [pltpu.SemaphoreType.DMA((size,))] * 6
     return pl.pallas_call(
-        border_kernel,
-        out_shape=jax.ShapeDtypeStruct(states.shape, f32),
-        compiler_params=pltpu.CompilerParams(vmem_limit_bytes=32 * 2**20),
-    )(states, maps)
+        lambda *refs: border_kernel(sizes, *refs),
+        in_specs=[pl.BlockSpec(memory_space=pltpu.VMEM)] * 4,
+        out_specs=pl.BlockSpec(memory_space=pltpu.VMEM),
+        out_shape=jax.ShapeDtypeStruct((2 * width, runs), f32),
+        scratch_shapes=scratch,
+        compiler_params=pltpu.CompilerParams(
+            collective_id=0, has_side_effects=True, vmem_limit_bytes=32 * 2**20
+        ),
+    )(end_state, first_state, end_map, first_map)
 
 
 def close_kernel(per, partial, maps, carries, smoothed, parts):
@@ -226,7 +331,7 @@
         out_specs=pl.BlockSpec((per, width, runs), along),
         out_shape=jax.ShapeDtypeStruct(partial.shape, f32),
         scratch_shapes=[pltpu.VMEM((3 * carries.shape[0], runs), bf16)],
-        compiler_params=pltpu.CompilerParams(vmem_limit_bytes=32 * 2**20),
+        compiler_params=pltpu.CompilerParams(vmem_limit_bytes=56 * 2**20),
     )(partial, maps, carries)
 
 
@@ -270,13 +375,7 @@
         process_noise, gauge_reads, weights, spread[:, None], retain[:, :, None],
         keep[:, :, None], map_parts(transition), map_parts(transition.T), transition,
     )
-    own = jnp.concatenate([end_state, first_state], axis=0)
-    own = own.reshape(2 * width, count, runs // count).transpose(1, 0, 2)
-    states = lax.all_to_all(own, "tm", 0, 0)
-    all_maps = lax.all_gather(jnp.concatenate([end_map, first_map], axis=1), "tm")
-    carries = border_pass(states, all_maps)
-    carries = lax.all_to_all(carries, "tm", 0, 0)
-    carries = carries.transpose(1, 0, 2).reshape(2 * width, runs)
+    carries = border_pass(end_state, first_state, end_map, first_map)
     return close_pass(partial, maps, carries)
 
 

time: 132 us -> 85.7 us (0.65)
  blocking collectives: 41 us -> 0 us
  Pallas kernels: 32.4 us -> 64.4 us
  waiting for transfers between devices: 19.2 us -> 0 us
  between operations: 16.2 us -> 2.8 us
  local copies, waits for them, and re-layouts: 10 us -> 6.23 us
    all_to_all x2 -> x0, blocking collectives: 41 us -> none  [the longest x1 23.1 us: shards(): states = lax.all_to_all(own, 'tm', 0, 0)]
    pallas_call x1, Pallas kernels: 4.29 us -> 32.3 us  [border_pass(): pl.pallas_call(lambda *refs: border_kernel(sizes, *refs), in_specs=[pl.Bl...]
    all_gather x1 -> x0, waiting for transfers between devices: 19.2 us -> none  [shards(): lax.all_gather(jnp.concatenate([end_map, first_map], axis=1), 'tm')]
    pallas_call x1, Pallas kernels: 7.39 us -> 11.3 us  [close_pass(): pl.pallas_call(body, grid=(steps // per,), in_specs=[pl.BlockSpec((per, w...]
    unnamed x4, local copies, waits for them, and re-layouts: 4.6 us -> 1.85 us
  transfers between devices with their start and end apart: 1 -> 0, of which waited for: 1 -> 0; matrix products, arithmetic and copies ran while one was open for 0% -> 0% of each run, Pallas kernels for 0% -> 0%
where the time goes in v2:
time: 85.7 us; the launch traced here: 85 us
  Pallas kernels  64.4 us (75%)
  other arithmetic  6.49 us (8%)
  local copies, waits for them, and re-layouts  6.23 us (7%)
  matrix products  5.05 us (6%)
  between operations  2.8 us (3%)
    pallas_call x1, Pallas kernels, border_pass(): pl.pallas_call(lambda *refs: border_kernel(sizes, *refs), in_specs=[pl.Bl...  32.3 us
    pallas_call x1, Pallas kernels, local_pass(): pl.pallas_call(body, grid=(2 * blocks,), in_specs=[pl.BlockSpec((per,) +...  20.8 us
    pallas_call x1, Pallas kernels, close_pass(): pl.pallas_call(body, grid=(steps // per,), in_specs=[pl.BlockSpec((per, w...  11.3 us
    dot_general x4, matrix products, rotation_basis(): jnp.dot(rotation, vector, precision=exact_mode)  3.55 us
    unnamed x4, local copies, waits for them, and re-layouts  1.85 us

profile of v2, /device:TPU:0, one launch (start us, length us, event | category | flops | bytes accessed | tf_op | source)
XLA Modules:
  0.0 85.0 jit_solution(17531429412317507301)
XLA Ops:
  0.0 0.8 convolution_bitcast_fusion.3
  0.8 0.7 broadcast_multiply_fusion
  1.5 0.7 cosine_multiply_fusion
  2.2 0.7 negate_log-plus-one_fusion
  2.9 1.5 %multiply_reduce_fusion = (f32[]{:T(128)}, f32[]{:T(128)}, f32[]{:T(128)}, f32[]{:T(128)}) fusion(f32[4,64]{1,0:T(4,128)} %param.12), kind=kLoop, calls=%fused_computation.79 | loop fusion | flops 508 | bytes 1040 | tf_op jit(solution)/shard_map/reduce_sum | solution.py:18
  7.1 0.8 slice_bitcast_fusion.3
  7.9 0.9 %convolution_bitcast_fusion.2 = f32[64]{0:T(128)S(1)} fusion(f32[64]{0:T(128)S(1)} %get-tuple-element.27, f32[64]{0:T(128)S(1)} %convolution_bitcast_fusion.3, f32[]{:T(128)S(6)} %div.18, f32[4,64]{1,0:T(4,128)} %param.12), kind=kOutput, calls=%fused_computation.4 | convolution fusion | flops 69632 | bytes 1284 | tf_op jit(solution)/shard_map/dot_general | solution.py:20
  8.8 0.9 %convolution_bitcast_fusion.1 = f32[64]{0:T(128)S(1)} fusion(f32[64]{0:T(128)S(1)} %get-tuple-element.28, f32[64]{0:T(128)S(1)} %convolution_bitcast_fusion.2, f32[]{:T(128)S(6)} %div.19, f32[64]{0:T(128)S(1)} %get-tuple-element.27, f32[64]{0:T(128)S(1)} %convolution_bitcast_fusion.3, f32[]{:T(128)S(6)} %div.18, f32[4,64]{1,0:T(4,128)} %param.12), kind=kOutput, calls=%fused_computation.3 | convolution fusion | flops 81920 | bytes 1800 | tf_op jit(solution)/shard_map/dot_general | solution.py:20
  9.8 0.9 %convolution_bitcast_fusion = f32[64]{0:T(128)S(1)} fusion(f32[64]{0:T(128)S(1)} %get-tuple-element.30, f32[64]{0:T(128)S(1)} %convolution_bitcast_fusion.1, f32[]{:T(128)S(6)} %div.20, f32[64]{0:T(128)S(1)} %get-tuple-element.28, f32[64]{0:T(128)S(1)} %convolution_bitcast_fusion.2, f32[]{:T(128)S(6)} %div.19, f32[64]{0:T(128)S(1)} %get-tuple-element.27, ...), kind=kOutput, calls=%fused_computation.2 | convolution fusion | flops 94208 | bytes 2316 | tf_op jit(solution)/shard_map/dot_general | solution.py:20
  10.7 0.8 convert_element_type.58
  11.5 0.9 %fusion = f32[64,32]{0,1:T(8,128)S(1)} fusion(s32[96]{0:T(128)S(1)} %broadcast_multiply_fusion, s32[32,96]{1,0:T(8,128)} %param.10, f32[64]{0:T(128)S(1)} %get-tuple-element.34), kind=kOutput, calls=%fused_computation.1 | convolution fusion | flops 2370560 | bytes 21120 | tf_op jit(solution)/shard_map/dot_general | solution.py:358
  12.6 0.1 broadcast_in_dim.79
  13.1 0.3 fusion.3
  13.4 0.3 fusion.1
  13.9 0.1 broadcast_in_dim.46
  14.1 0.2 multiply_multiply_fusion.1
  14.2 1.6 %pad_maximum_fusion.refs_2_ = bf16[32,64,256]{2,1,0:T(8,128)(2,1)} fusion(bf16[32,64,96]{2,1,0:T(8,128)(2,1)S(1)} %get-tuple-element.26, bf16[32,64,96]{2,1,0:T(8,128)(2,1)S(1)} %get-tuple-element.25, bf16[32,64,64]{2,1,0:T(8,128)(2,1)S(1)} %broadcast_in_dim.46), kind=kLoop, calls=%fused_computation.6 | loop fusion | flops 3145728 | bytes 2097152 | tf_op jit(solution)/shard_map/concatenate | solution.py:366
  15.8 1.4 %copy.18.refs_5_ = f32[32,64,1]{2,1,0:T(8,128)} copy(f32[32,64,1]{1,0,2:T(8,128)S(1)} %fusion.9) | data formatting | bytes 16384 | tf_op jit(solution)/shard_map/broadcast_in_dim | solution.py:376
  17.2 1.5 %copy.17.refs_4_ = f32[32,64,1]{2,1,0:T(8,128)} copy(f32[32,64,1]{1,0,2:T(8,128)S(1)} %bitcast.48) | data formatting | bytes 16384 | tf_op jit(solution)/shard_map/broadcast_in_dim | solution.py:375
  18.7 20.8 %shard_map.82 = (f32[32,64,1024]{2,1,0:T(8,128)}, f32[32,64,128]{2,1,0:T(8,128)S(1)}, f32[64,1024]{1,0:T(8,128)S(1)}, f32[64,128]{1,0:T(8,128)S(1)}, f32[64,1024]{1,0:T(8,128)S(1)}, /*index=5*/f32[64,128]{1,0:T(8,128)S(1)}) custom-call(bf16[32,64,1024]{2,1,0:T(8,128)(2,1)} %refs_0_.1, bf16[32,96,1024]{2,1,0:T(8,128)(2,1)} %refs_1_.1, ...), custom_call_target="tpu_custom_call" | custom-call | tf_op jit(solution)/shard_map/pallas_call | solution.py:133
  39.5 1.1 %copy-done.1 = f32[32,64,128]{2,1,0:T(8,128)} copy-done((f32[32,64,128]{2,1,0:T(8,128)}, f32[32,64,128]{2,1,0:T(8,128)S(1)}, u32[]{:S(2)}) %copy-start.1) | copy-done | bytes 1048600
  40.6 32.3 %shard_map.83.refs_2_ = f32[128,1024]{1,0:T(8,128)S(1)} custom-call(f32[64,1024]{1,0:T(8,128)S(1)} %get-tuple-element.13.refs_0_, f32[64,1024]{1,0:T(8,128)S(1)} %get-tuple-element.14.refs_1_, f32[64,128]{1,0:T(8,128)S(1)} %get-tuple-element.15.refs_2_, f32[64,128]{1,0:T(8,128)S(1)} %get-tuple-element.16.refs_3_), custom_call_target="tpu_custom_call" | custom-call | tf_op jit(solution)/shard_map/pallas_call | solution.py:294
  72.9 0.8 copy-done
  73.6 11.3 %shard_map.84 = f32[32,64,1024]{2,1,0:T(8,128)} custom-call(f32[32,64,1024]{2,1,0:T(8,128)} %get-tuple-element.11.refs_0_, f32[32,64,128]{2,1,0:T(8,128)} %copy-done.1, f32[128,1024]{1,0:T(8,128)} %copy-done), custom_call_target="tpu_custom_call" | custom-call | tf_op jit(solution)/shard_map/pallas_call | solution.py:323
  (17 shorter events, 0.9 us)
Async XLA Ops:
  39.5 1.1 %copy-start.1 = (f32[32,64,128]{2,1,0:T(8,128)}, f32[32,64,128]{2,1,0:T(8,128)S(1)}, u32[]{:S(2)}) copy-start(f32[32,64,128]{2,1,0:T(8,128)S(1)} %get-tuple-element.12.refs_1_) | copy-start | bytes 3145732
  72.9 0.8 copy-start

commit v3 on v2

--- a/solution.py
+++ b/solution.py
@@ -10,42 +10,74 @@
 f32 = jnp.float32
 
 
-def rotation_basis(reflectors):
-    width_all = reflectors.shape[1]
-    rotation = jnp.eye(width_all, dtype=f32)
-    for number in range(reflectors.shape[0]):
-        vector = reflectors[number]
-        factor = 2.0 / (jnp.sum(vector * vector) + 1e-06)
-        rotation = rotation - factor * jnp.outer(
-            jnp.dot(rotation, vector, precision=exact_mode), vector
-        )
-    return rotation
-
-
-def pair_blocks(decay_rates, turn_angles):
-    radius = jnp.exp(-decay_rates)
-    cosine = jnp.repeat(radius * jnp.cos(turn_angles), 2)
-    sine_part = jnp.repeat(radius * jnp.sin(turn_angles), 2)
-    positions = jnp.arange(cosine.shape[0])
-    pair_index = positions // 2
-    parity = positions % 2
-    same_pair = pair_index[:, None] == pair_index[None, :]
-    same_parity = parity[:, None] == parity[None, :]
-    upper = parity[:, None] == 0
-    element = jnp.where(
-        same_parity, cosine[:, None], jnp.where(upper, -sine_part[:, None], sine_part[:, None])
-    )
-    return jnp.where(same_pair, element, 0.0)
-
-
 def two_parts(x):
-    high = lax.reduce_precision(x, 8, 7)
-    return high.astype(bf16), (x - high).astype(bf16)
+    high = x.astype(bf16)
+    return high, (x - high.astype(f32)).astype(bf16)
 
 
 def map_parts(matrix):
     high, low = two_parts(matrix)
     return jnp.concatenate([high, low, high], axis=1)
+
+
+def index_of(shape):
+    return lax.broadcasted_iota(jnp.int32, shape, 0), lax.broadcasted_iota(jnp.int32, shape, 1)
+
+
+def as_column(line):
+    row, col = index_of((line.shape[1], line.shape[1]))
+    return jnp.sum(jnp.where(row == col, line, 0.0), axis=1, keepdims=True)
+
+
+def pair_column(line):
+    row, col = index_of((2 * line.shape[1], line.shape[1]))
+    return jnp.sum(jnp.where(row // 2 == col, line, 0.0), axis=1, keepdims=True)
+
+
+def across(a, b, precision=None):
+    return lax.dot_general(
+        a, b, (((1,), (1,)), ((), ())), precision=precision, preferred_element_type=f32
+    )
+
+
+def prepare(
+    active, link, reflectors, decay, turn, gain, scale,
+    spread, retain, fwd_map, bwd_map, trans, base, mask,
+):
+    steps = active.shape[0]
+    width = trans.shape[0]
+    row, col = index_of((width, width))
+    rotation = jnp.where(row == col, 1.0, 0.0)
+    for number in range(reflectors.shape[0]):
+        vector = reflectors[number : number + 1, :]
+        factor = 2.0 / (jnp.sum(vector * vector, axis=1, keepdims=True) + 1e-06)
+        hit = jnp.sum(rotation * vector, axis=1, keepdims=True)
+        rotation = rotation - factor * (hit * vector)
+    decays, turns = pair_column(decay[...]), pair_column(turn[...])
+    radius = jnp.exp(-decays)
+    cosine, sine = radius * jnp.cos(turns), radius * jnp.sin(turns)
+    element = jnp.where(row % 2 == col % 2, cosine, jnp.where(row % 2 == 0, -sine, sine))
+    blocks = jnp.where(row // 2 == col // 2, element, 0.0)
+    turned = jnp.dot(rotation, blocks, precision=exact_mode, preferred_element_type=f32)
+    transition = across(turned, rotation, exact_mode)
+    trans[...] = transition
+    fwd_map[...] = map_parts(transition)
+    bwd_map[...] = map_parts(transition.T)
+    spread[...] = pair_column(scale[...])
+    gains = as_column(gain[...])
+    gauge_row, _ = index_of((width, link.shape[1]))
+    placed = jnp.where(gauge_row == 2 * link[...], 1.0, 0.0)
+    on = active[...].astype(f32)
+    counts = across(placed.astype(bf16), on.astype(bf16))
+    rates = jnp.exp(counts * jnp.log1p(-gains))
+    for t in range(steps):
+        retain[t] = rates[:, t : t + 1]
+    high, low = two_parts(gains)
+    base[...] = jnp.concatenate(
+        [rotation.astype(bf16).astype(f32), high.astype(f32) * placed, low.astype(f32) * placed],
+        axis=1,
+    )
+    mask[...] = jnp.concatenate([jnp.ones((steps, width), f32), on, on], axis=1)
 
 
 def state_parts(x):
@@ -59,17 +91,22 @@
 
 
 def local_kernel(
-    blocks, per, noise, gauges, weights, spread, retain, keep, fwd_map, bwd_map, trans,
+    blocks, per, noise, gauges, active, link, reflectors, decay, turn, gain, scale,
     partial, maps, end_state, end_map, first_state, first_map,
-    filt, filt_x, pred, pred_x, run, run_x,
+    filt, filt_x, pred, pred_x, run, run_x, spread, retain, fwd_map, bwd_map, trans, base, mask,
 ):
     step = pl.program_id(0)
     width = trans.shape[0]
+    final_device = lax.axis_index("tm") == lax.axis_size("tm") - 1
 
     @pl.when(step == 0)
     def _():
+        prepare(
+            active, link, reflectors, decay, turn, gain, scale,
+            spread, retain, fwd_map, bwd_map, trans, base, mask,
+        )
         run[...] = jnp.zeros_like(run)
-        run_x[...] = jnp.concatenate([trans[...], jnp.zeros_like(trans)], axis=1)
+        run_x[...] = jnp.concatenate([trans[...], jnp.zeros(trans.shape, f32)], axis=1)
 
     @pl.when(step < blocks)
     def _():
@@ -78,7 +115,8 @@
             t = step * per + i
             scaled = (spread[...] * noise[i].astype(f32)).astype(bf16)
             reads = gauges[i]
-            offset = dot32(weights[i], jnp.concatenate([scaled, reads, reads], axis=0))
+            weights = (base[...] * mask[pl.ds(t, 1), :]).astype(bf16)
+            offset = dot32(weights, jnp.concatenate([scaled, reads, reads], axis=0))
             rate = retain[t]
             f = rate * p + offset
             fx = rate * px
@@ -95,6 +133,7 @@
         def _():
             end_state[...] = f
             end_map[...] = fx
+            retain[t] = jnp.where(final_device, 0.0, rate)
             run[...] = jnp.zeros_like(run)
             row = lax.broadcasted_iota(jnp.int32, run_x.shape, 0)
             col = lax.broadcasted_iota(jnp.int32, run_x.shape, 1)
@@ -105,7 +144,7 @@
         s, sx = run[...], run_x[...]
         for i in reversed(range(per)):
             t = (2 * blocks - 1 - step) * per + i
-            rate = keep[t]
+            rate = retain[t]
             s = filt[t] + dot32(bwd_map[...], state_parts(rate * (s - pred[t])))
             sx = filt_x[t] + dot32(bwd_map[...], state_parts(rate * (sx - pred_x[t])))
             partial[i] = s
@@ -119,7 +158,7 @@
             first_map[...] = sx
 
 
-def local_pass(noise, gauges, weights, spread, retain, keep, fwd_map, bwd_map, trans):
+def local_pass(noise, gauges, *terms):
     steps, width, runs = noise.shape
     per = 4
     blocks = steps // per
@@ -136,8 +175,7 @@
         in_specs=[
             pl.BlockSpec((per,) + noise.shape[1:], ahead),
             pl.BlockSpec((per,) + gauges.shape[1:], ahead),
-            pl.BlockSpec((per,) + weights.shape[1:], ahead),
-            full(spread), full(retain), full(keep), full(fwd_map), full(bwd_map), full(trans),
+            *[full(x) for x in terms],
         ],
         out_specs=[
             pl.BlockSpec((per, width, runs), back),
@@ -162,9 +200,16 @@
             pltpu.VMEM((steps, width, extra), f32),
             pltpu.VMEM((width, runs), f32),
             pltpu.VMEM((width, extra), f32),
+            pltpu.VMEM((width, 1), f32),
+            pltpu.VMEM((steps, width, 1), f32),
+            pltpu.VMEM((width, 3 * width), bf16),
+            pltpu.VMEM((width, 3 * width), bf16),
+            pltpu.VMEM((width, width), f32),
+            pltpu.VMEM((width, width + 2 * gauges.shape[1]), f32),
+            pltpu.VMEM((steps, width + 2 * gauges.shape[1]), f32),
         ],
         compiler_params=pltpu.CompilerParams(vmem_limit_bytes=52 * 2**20),
-    )(noise, gauges, weights, spread, retain, keep, fwd_map, bwd_map, trans)
+    )(noise, gauges, *terms)
 
 
 def split_dot(matrix, state):
@@ -331,7 +376,7 @@
         out_specs=pl.BlockSpec((per, width, runs), along),
         out_shape=jax.ShapeDtypeStruct(partial.shape, f32),
         scratch_shapes=[pltpu.VMEM((3 * carries.shape[0], runs), bf16)],
-        compiler_params=pltpu.CompilerParams(vmem_limit_bytes=56 * 2**20),
+        compiler_params=pltpu.CompilerParams(vmem_limit_bytes=32 * 2**20),
     )(partial, maps, carries)
 
 
@@ -345,35 +390,10 @@
     turn_angles,
     gauge_gain,
 ):
-    steps, width, runs = process_noise.shape
-    count = lax.axis_size("tm")
-    rotation = rotation_basis(reflectors)
-    blocks = pair_blocks(decay_rates, turn_angles)
-    transition = jnp.dot(
-        jnp.dot(rotation, blocks, precision=exact_mode), rotation.T, precision=exact_mode
-    )
-    positions = jnp.arange(width)
-    onehot = (positions[None, :] == 2 * sensor_link[:, None]).astype(f32)
-    active = sensor_active.astype(f32)
-    counts = jnp.dot(active, onehot, precision=exact_mode)
-    retain = jnp.exp(counts * jnp.log1p(-gauge_gain)[None, :])
-    spread = jnp.repeat(jnp.sqrt(-jnp.expm1(-2.0 * decay_rates)), 2)
-    last_row = (jnp.arange(steps) == steps - 1)[:, None]
-    final_device = lax.axis_index("tm") == count - 1
-    keep = jnp.where(jnp.logical_and(last_row, final_device), 0.0, retain)
-    gain_high, gain_low = two_parts(gauge_gain)
-    placed = (onehot.T.astype(bf16))[None] * sensor_active.astype(bf16)[:, None, :]
-    weights = jnp.concatenate(
-        [
-            jnp.broadcast_to(rotation.astype(bf16)[None], (steps, width, width)),
-            gain_high[None, :, None] * placed,
-            gain_low[None, :, None] * placed,
-        ],
-        axis=2,
-    )
     partial, maps, end_state, end_map, first_state, first_map = local_pass(
-        process_noise, gauge_reads, weights, spread[:, None], retain[:, :, None],
-        keep[:, :, None], map_parts(transition), map_parts(transition.T), transition,
+        process_noise, gauge_reads, sensor_active, sensor_link[None], reflectors,
+        decay_rates[None], turn_angles[None], gauge_gain[None],
+        jnp.sqrt(-jnp.expm1(-2.0 * decay_rates))[None],
     )
     carries = border_pass(end_state, first_state, end_map, first_map)
     return close_pass(partial, maps, carries)

time: 85.7 us -> 69.1 us (0.81)
  other arithmetic: 6.49 us -> 0.67 us
  matrix products: 5.05 us -> 0 us
  Pallas kernels: 64.4 us -> 60.6 us
  between operations: 2.8 us -> 0.03 us
  local copies, waits for them, and re-layouts: 6.23 us -> 7.4 us
    unnamed x4 -> x14, local copies, waits for them, and re-layouts: 1.85 us -> 7.4 us
    dot_general x7 -> x0, matrix products: 5.05 us -> none  [the longest x4 3.55 us: rotation_basis(): jnp.dot(rotation, vector, precision=exact_mode)]
    pallas_call x1, Pallas kernels: 11.3 us -> 7.42 us  [close_pass(): pl.pallas_call(body, grid=(steps // per,), in_specs=[pl.BlockSpec((per, w...]
    broadcast_in_dim x7 -> x0, local copies, waits for them, and re-layouts: 3.29 us -> none  [the longest x1 1.48 us: shards(): retain[:, :, None]]
    concatenate x3 -> x0, other arithmetic: 1.76 us -> none  [the longest x1 1.59 us: shards(): jnp.concatenate([jnp.broadcast_to(rotation.astype(bf16)[None], (steps, wi...]
    mul x3 -> x0, other arithmetic: 1.58 us -> none  [the longest x1 0.71 us: pair_blocks(): cosine = jnp.repeat(radius * jnp.cos(turn_angles), 2)]
    reduce_sum x1 -> x0, other arithmetic: 1.52 us -> none  [rotation_basis(): factor = 2.0 / (jnp.sum(vector * vector) + 1e-06)]
    convert_element_type x4 -> x0, other arithmetic: 0.88 us -> none  [the longest x1 0.75 us: shards(): sensor_active.astype(bf16)[:, None, :]]
where the time goes in v3:
time: 69.1 us; the launch traced here: 68.7 us
  Pallas kernels  60.6 us (88%)
  local copies, waits for them, and re-layouts  7.4 us (11%)
    pallas_call x1, Pallas kernels, border_pass(): pl.pallas_call(lambda *refs: border_kernel(sizes, *refs), in_specs=[pl.Bl...  32.3 us
    pallas_call x1, Pallas kernels, local_pass(): pl.pallas_call(body, grid=(2 * blocks,), in_specs=[pl.BlockSpec((per,) +...  20.9 us
    pallas_call x1, Pallas kernels, close_pass(): pl.pallas_call(body, grid=(steps // per,), in_specs=[pl.BlockSpec((per, w...  7.42 us
    unnamed x14, local copies, waits for them, and re-layouts  7.4 us

profile of v3, /device:TPU:0, one launch (start us, length us, event | category | flops | bytes accessed | tf_op | source)
XLA Modules:
  0.0 68.7 jit_solution(18336479476299654527)
XLA Ops:
  0.0 0.7 sqrt_bitcast_fusion.refs_8_
  0.7 0.0 copy-start.1
  0.7 0.7 %copy-done.1 = s32[32,96]{1,0:T(8,128)S(1)} copy-done((s32[32,96]{1,0:T(8,128)S(1)}, s32[32,96]{1,0:T(8,128)}, u32[]{:S(2)}) %copy-start.1) | copy-done | bytes 12312
  1.4 0.0 copy-start.2
  1.4 0.7 copy-done.2
  2.1 0.0 copy-start.3
  2.1 0.7 copy-done.3
  2.7 0.0 copy-start.4
  2.7 0.7 copy-done.4
  3.4 0.0 copy-start.5
  3.4 0.7 copy-done.5
  4.0 0.0 copy-start.6
  4.0 0.7 copy-done.6
  4.7 20.9 %shard_map.82 = (f32[32,64,1024]{2,1,0:T(8,128)}, f32[32,64,128]{2,1,0:T(8,128)S(1)}, f32[64,1024]{1,0:T(8,128)S(1)}, f32[64,128]{1,0:T(8,128)S(1)}, f32[64,1024]{1,0:T(8,128)S(1)}, /*index=5*/f32[64,128]{1,0:T(8,128)S(1)}) custom-call(bf16[32,64,1024]{2,1,0:T(8,128)(2,1)} %refs_0_.1, bf16[32,96,1024]{2,1,0:T(8,128)(2,1)} %refs_1_.1, ...), custom_call_target="tpu_custom_call" | custom-call | tf_op jit(solution)/shard_map/pallas_call | solution.py:172
  25.6 32.3 %shard_map.83.refs_2_ = f32[128,1024]{1,0:T(8,128)S(1)} custom-call(f32[64,1024]{1,0:T(8,128)S(1)} %get-tuple-element.13.refs_0_, f32[64,1024]{1,0:T(8,128)S(1)} %get-tuple-element.14.refs_1_, f32[64,128]{1,0:T(8,128)S(1)} %get-tuple-element.15.refs_2_, f32[64,128]{1,0:T(8,128)S(1)} %get-tuple-element.16.refs_3_), custom_call_target="tpu_custom_call" | custom-call | tf_op jit(solution)/shard_map/pallas_call | solution.py:339
  57.9 0.0 copy-start
  57.9 3.4 %copy-done = f32[32,64,1024]{2,1,0:T(8,128)S(1)} copy-done((f32[32,64,1024]{2,1,0:T(8,128)S(1)}, f32[32,64,1024]{2,1,0:T(8,128)}, u32[]{:S(2)}) %copy-start) | copy-done | bytes 8388632
  61.2 7.4 %shard_map.84 = f32[32,64,1024]{2,1,0:T(8,128)} custom-call(f32[32,64,1024]{2,1,0:T(8,128)S(1)} %copy-done, f32[32,64,128]{2,1,0:T(8,128)S(1)} %get-tuple-element.12.refs_1_, f32[128,1024]{1,0:T(8,128)S(1)} %shard_map.83.refs_2_), custom_call_target="tpu_custom_call" | custom-call | tf_op jit(solution)/shard_map/pallas_call | solution.py:368
Async XLA Ops:
  0.7 0.7 %copy-start.1 = (s32[32,96]{1,0:T(8,128)S(1)}, s32[32,96]{1,0:T(8,128)}, u32[]{:S(2)}) copy-start(s32[32,96]{1,0:T(8,128)} %refs_2_.1) | copy-start | bytes 36868
  1.4 0.7 copy-start.2
  2.1 0.7 copy-start.3
  2.7 0.7 copy-start.4
  3.4 0.7 copy-start.5
  4.0 0.7 copy-start.6
  57.9 3.4 %copy-start = (f32[32,64,1024]{2,1,0:T(8,128)S(1)}, f32[32,64,1024]{2,1,0:T(8,128)}, u32[]{:S(2)}) copy-start(f32[32,64,1024]{2,1,0:T(8,128)} %get-tuple-element.11.refs_0_) | copy-start | bytes 25165828

commit v4 on v3

--- a/solution.py
+++ b/solution.py
@@ -147,7 +147,7 @@
             rate = retain[t]
             s = filt[t] + dot32(bwd_map[...], state_parts(rate * (s - pred[t])))
             sx = filt_x[t] + dot32(bwd_map[...], state_parts(rate * (sx - pred_x[t])))
-            partial[i] = s
+            partial[i] = s.astype(bf16)
             maps[i] = sx
         run[...] = s
         run_x[...] = sx
@@ -186,7 +186,7 @@
             pl.BlockSpec((width, extra), whole2),
         ],
         out_shape=[
-            jax.ShapeDtypeStruct((steps, width, runs), f32),
+            jax.ShapeDtypeStruct((steps, width, runs), bf16),
             jax.ShapeDtypeStruct((steps, width, extra), f32),
             jax.ShapeDtypeStruct((width, runs), f32),
             jax.ShapeDtypeStruct((width, extra), f32),
@@ -208,7 +208,7 @@
             pltpu.VMEM((width, width + 2 * gauges.shape[1]), f32),
             pltpu.VMEM((steps, width + 2 * gauges.shape[1]), f32),
         ],
-        compiler_params=pltpu.CompilerParams(vmem_limit_bytes=52 * 2**20),
+        compiler_params=pltpu.CompilerParams(vmem_limit_bytes=62 * 2**20),
     )(noise, gauges, *terms)
 
 
@@ -357,7 +357,7 @@
         m = maps[i]
         high = m.astype(bf16)
         low = (m - high.astype(f32)).astype(bf16)
-        smoothed[i] = partial[i] + dot32(jnp.concatenate([high, low, high], axis=1), parts[...])
+        smoothed[i] = partial[i].astype(f32) + dot32(jnp.concatenate([high, low, high], axis=1), parts[...])
 
 
 def close_pass(partial, maps, carries):

time: 69.1 us -> 69.5 us (level)
    unnamed x14 -> x12, local copies, waits for them, and re-layouts: 7.4 us -> 6.81 us
where the time goes in v4:
time: 69.5 us; the launch traced here: 69 us
  Pallas kernels  61 us (88%)
  local copies, waits for them, and re-layouts  6.81 us (10%)
  other arithmetic  1.16 us (2%)
    pallas_call x1, Pallas kernels, border_pass(): pl.pallas_call(lambda *refs: border_kernel(sizes, *refs), in_specs=[pl.Bl...  32.3 us
    pallas_call x1, Pallas kernels, local_pass(): pl.pallas_call(body, grid=(2 * blocks,), in_specs=[pl.BlockSpec((per,) +...  21.3 us
    pallas_call x1, Pallas kernels, close_pass(): pl.pallas_call(body, grid=(steps // per,), in_specs=[pl.BlockSpec((per, w...  7.39 us
    unnamed x12, local copies, waits for them, and re-layouts  6.81 us

profile of v4, /device:TPU:0, one launch (start us, length us, event | category | flops | bytes accessed | tf_op | source)
XLA Modules:
  0.0 69.0 jit_solution(13330337750004838127)
XLA Ops:
  0.0 1.2 %sqrt_bitcast_fusion.refs_8_ = f32[1,32]{1,0:T(1,128)} fusion(f32[32]{0:T(128)} %param.13), kind=kLoop, calls=%fused_computation | loop fusion | flops 64 | bytes 256 | tf_op jit(solution)/shard_map/broadcast_in_dim | solution.py:396
  1.2 21.3 %shard_map.82 = (bf16[32,64,1024]{2,1,0:T(8,128)(2,1)}, f32[32,64,128]{2,1,0:T(8,128)}, f32[64,1024]{1,0:T(8,128)}, f32[64,128]{1,0:T(8,128)}, f32[64,1024]{1,0:T(8,128)}, /*index=5*/f32[64,128]{1,0:T(8,128)}) custom-call(bf16[32,64,1024]{2,1,0:T(8,128)(2,1)} %refs_0_.1, bf16[32,96,1024]{2,1,0:T(8,128)(2,1)} %refs_1_.1, s32[32,96]{1,0:T(8,128)} %refs_2_.1, ...), custom_call_target="tpu_custom_call" | custom-call | tf_op jit(solution)/shard_map/pallas_call | solution.py:172
  22.5 0.0 copy-start.2
  22.5 0.9 %copy-done.2 = f32[64,1024]{1,0:T(8,128)S(1)} copy-done((f32[64,1024]{1,0:T(8,128)S(1)}, f32[64,1024]{1,0:T(8,128)}, u32[]{:S(2)}) %copy-start.2) | copy-done | bytes 262168
  23.4 0.0 copy-start.3
  23.4 0.9 %copy-done.3 = f32[64,1024]{1,0:T(8,128)S(1)} copy-done((f32[64,1024]{1,0:T(8,128)S(1)}, f32[64,1024]{1,0:T(8,128)}, u32[]{:S(2)}) %copy-start.3) | copy-done | bytes 262168
  24.4 0.0 copy-start.4
  24.4 0.8 %copy-done.4 = f32[64,128]{1,0:T(8,128)S(1)} copy-done((f32[64,128]{1,0:T(8,128)S(1)}, f32[64,128]{1,0:T(8,128)}, u32[]{:S(2)}) %copy-start.4) | copy-done | bytes 32792
  25.1 0.0 copy-start.5
  25.1 0.8 %copy-done.5 = f32[64,128]{1,0:T(8,128)S(1)} copy-done((f32[64,128]{1,0:T(8,128)S(1)}, f32[64,128]{1,0:T(8,128)}, u32[]{:S(2)}) %copy-start.5) | copy-done | bytes 32792
  25.9 32.3 %shard_map.83.refs_2_ = f32[128,1024]{1,0:T(8,128)S(1)} custom-call(f32[64,1024]{1,0:T(8,128)S(1)} %copy-done.2, f32[64,1024]{1,0:T(8,128)S(1)} %copy-done.3, f32[64,128]{1,0:T(8,128)S(1)} %copy-done.4, f32[64,128]{1,0:T(8,128)S(1)} %copy-done.5), custom_call_target="tpu_custom_call" | custom-call | tf_op jit(solution)/shard_map/pallas_call | solution.py:339
  58.2 0.0 copy-start
  58.2 2.2 %copy-done = bf16[32,64,1024]{2,1,0:T(8,128)(2,1)S(1)} copy-done((bf16[32,64,1024]{2,1,0:T(8,128)(2,1)S(1)}, bf16[32,64,1024]{2,1,0:T(8,128)(2,1)}, u32[]{:S(2)}) %copy-start) | copy-done | bytes 4194328
  60.4 0.0 copy-start.1
  60.4 1.2 %copy-done.1 = f32[32,64,128]{2,1,0:T(8,128)S(1)} copy-done((f32[32,64,128]{2,1,0:T(8,128)S(1)}, f32[32,64,128]{2,1,0:T(8,128)}, u32[]{:S(2)}) %copy-start.1) | copy-done | bytes 1048600
  61.6 7.4 %shard_map.84 = f32[32,64,1024]{2,1,0:T(8,128)} custom-call(bf16[32,64,1024]{2,1,0:T(8,128)(2,1)S(1)} %copy-done, f32[32,64,128]{2,1,0:T(8,128)S(1)} %copy-done.1, f32[128,1024]{1,0:T(8,128)S(1)} %shard_map.83.refs_2_), custom_call_target="tpu_custom_call" | custom-call | tf_op jit(solution)/shard_map/pallas_call | solution.py:368
Async XLA Ops:
  22.5 1.0 %copy-start.2 = (f32[64,1024]{1,0:T(8,128)S(1)}, f32[64,1024]{1,0:T(8,128)}, u32[]{:S(2)}) copy-start(f32[64,1024]{1,0:T(8,128)} %get-tuple-element.13.refs_0_) | copy-start | bytes 786436
  23.4 0.9 %copy-start.3 = (f32[64,1024]{1,0:T(8,128)S(1)}, f32[64,1024]{1,0:T(8,128)}, u32[]{:S(2)}) copy-start(f32[64,1024]{1,0:T(8,128)} %get-tuple-element.14.refs_1_) | copy-start | bytes 786436
  24.4 0.8 %copy-start.4 = (f32[64,128]{1,0:T(8,128)S(1)}, f32[64,128]{1,0:T(8,128)}, u32[]{:S(2)}) copy-start(f32[64,128]{1,0:T(8,128)} %get-tuple-element.15.refs_2_) | copy-start | bytes 98308
  25.1 0.8 %copy-start.5 = (f32[64,128]{1,0:T(8,128)S(1)}, f32[64,128]{1,0:T(8,128)}, u32[]{:S(2)}) copy-start(f32[64,128]{1,0:T(8,128)} %get-tuple-element.16.refs_3_) | copy-start | bytes 98308
  58.2 2.2 %copy-start = (bf16[32,64,1024]{2,1,0:T(8,128)(2,1)S(1)}, bf16[32,64,1024]{2,1,0:T(8,128)(2,1)}, u32[]{:S(2)}) copy-start(bf16[32,64,1024]{2,1,0:T(8,128)(2,1)} %get-tuple-element.11.refs_0_) | copy-start | bytes 12582916
  60.4 1.2 %copy-start.1 = (f32[32,64,128]{2,1,0:T(8,128)S(1)}, f32[32,64,128]{2,1,0:T(8,128)}, u32[]{:S(2)}) copy-start(f32[32,64,128]{2,1,0:T(8,128)} %get-tuple-element.12.refs_1_) | copy-start | bytes 3145732

commit v5 on v4

--- a/solution.py
+++ b/solution.py
@@ -91,7 +91,7 @@
 
 
 def local_kernel(
-    blocks, per, noise, gauges, active, link, reflectors, decay, turn, gain, scale,
+    blocks, per, noise, gauges, active, link, reflectors, lines,
     partial, maps, end_state, end_map, first_state, first_map,
     filt, filt_x, pred, pred_x, run, run_x, spread, retain, fwd_map, bwd_map, trans, base, mask,
 ):
@@ -101,6 +101,9 @@
 
     @pl.when(step == 0)
     def _():
+        half = width // 2
+        decay, turn, scale = (lines[j : j + 1, :half] for j in range(3))
+        gain = lines[3:4, :]
         prepare(
             active, link, reflectors, decay, turn, gain, scale,
             spread, retain, fwd_map, bwd_map, trans, base, mask,
@@ -208,7 +211,7 @@
             pltpu.VMEM((width, width + 2 * gauges.shape[1]), f32),
             pltpu.VMEM((steps, width + 2 * gauges.shape[1]), f32),
         ],
-        compiler_params=pltpu.CompilerParams(vmem_limit_bytes=62 * 2**20),
+        compiler_params=pltpu.CompilerParams(vmem_limit_bytes=52 * 2**20),
     )(noise, gauges, *terms)
 
 
@@ -390,10 +393,11 @@
     turn_angles,
     gauge_gain,
 ):
+    scale = jnp.sqrt(-jnp.expm1(-2.0 * decay_rates))
+    wide = jnp.tile(jnp.stack([decay_rates, turn_angles, scale]), (1, 2))
     partial, maps, end_state, end_map, first_state, first_map = local_pass(
         process_noise, gauge_reads, sensor_active, sensor_link[None], reflectors,
-        decay_rates[None], turn_angles[None], gauge_gain[None],
-        jnp.sqrt(-jnp.expm1(-2.0 * decay_rates))[None],
+        jnp.concatenate([wide, gauge_gain[None]], axis=0),
     )
     carries = border_pass(end_state, first_state, end_map, first_map)
     return close_pass(partial, maps, carries)

time: 69.5 us -> 67.2 us (0.967)
  local copies, waits for them, and re-layouts: 6.81 us -> 4.33 us
  other arithmetic: 1.16 us -> 2.02 us
    unnamed x12 -> x8, local copies, waits for them, and re-layouts: 6.81 us -> 4.24 us
    another operation x0 -> x2, other arithmetic: none -> 1.36 us  [shards(): wide = jnp.tile(jnp.stack([decay_rates, turn_angles, scale]), (1, 2))]
    broadcast_in_dim x1 -> x0, other arithmetic: 1.16 us -> none  [shards(): jnp.sqrt(-jnp.expm1(-2.0 * decay_rates))[None]]
where the time goes in v5:
time: 67.2 us; the launch traced here: 66.8 us
  Pallas kernels  60.4 us (90%)
  local copies, waits for them, and re-layouts  4.33 us (6%)
  other arithmetic  2.02 us (3%)
    pallas_call x1, Pallas kernels, border_pass(): pl.pallas_call(lambda *refs: border_kernel(sizes, *refs), in_specs=[pl.Bl...  32.3 us
    pallas_call x1, Pallas kernels, local_pass(): pl.pallas_call(body, grid=(2 * blocks,), in_specs=[pl.BlockSpec((per,) +...  20.7 us
    pallas_call x1, Pallas kernels, close_pass(): pl.pallas_call(body, grid=(steps // per,), in_specs=[pl.BlockSpec((per, w...  7.41 us
    unnamed x8, local copies, waits for them, and re-layouts  4.24 us
    another operation x2, other arithmetic, shards(): wide = jnp.tile(jnp.stack([decay_rates, turn_angles, scale]), (1, 2))  1.36 us

profile of v5, /device:TPU:0, one launch (start us, length us, event | category | flops | bytes accessed | tf_op | source)
XLA Modules:
  0.0 66.8 jit_solution(961244705971399879)
XLA Ops:
  0.0 0.7 sqrt_bitcast_fusion
  0.7 0.7 %pad_maximum_fusion = f32[3,32]{1,0:T(4,128)S(1)} fusion(f32[1,32]{1,0:T(1,128)S(1)} %sqrt_bitcast_fusion, f32[1,32]{1,0:T(1,128)} %bitcast.8, f32[1,32]{1,0:T(1,128)} %bitcast.7), kind=kLoop, calls=%fused_computation | loop fusion | flops 192 | bytes 768 | tf_op jit(solution)/shard_map/stack | solution.py:397
  1.4 0.1 tile.10
  1.4 0.7 pad_maximum_fusion.1.refs_5_
  2.1 0.0 copy-start.1
  2.1 0.7 %copy-done.1 = s32[32,96]{1,0:T(8,128)S(1)} copy-done((s32[32,96]{1,0:T(8,128)S(1)}, s32[32,96]{1,0:T(8,128)}, u32[]{:S(2)}) %copy-start.1) | copy-done | bytes 12312
  2.8 0.0 copy-start.2
  2.8 0.7 %copy-done.2 = f32[4,64]{1,0:T(4,128)S(1)} copy-done((f32[4,64]{1,0:T(4,128)S(1)}, f32[4,64]{1,0:T(4,128)}, u32[]{:S(2)}) %copy-start.2) | copy-done | bytes 1048
  3.5 0.0 copy-start.3
  3.5 0.7 copy-done.3
  4.2 20.7 %shard_map.82 = (bf16[32,64,1024]{2,1,0:T(8,128)(2,1)}, f32[32,64,128]{2,1,0:T(8,128)S(1)}, f32[64,1024]{1,0:T(8,128)S(1)}, f32[64,128]{1,0:T(8,128)S(1)}, f32[6...) custom-call(bf16[32,64,1024]{2,1,0:T(8,128)(2,1)} %refs_0_.1, bf16[32,96,1024]{2,1,0:T(8,128)(2,1)} %refs_1_.1, ...), custom_call_target="tpu_custom_call" | custom-call | tf_op jit(solution)/shard_map/pallas_call | solution.py:175
  24.9 32.3 %shard_map.83.refs_2_ = f32[128,1024]{1,0:T(8,128)S(1)} custom-call(f32[64,1024]{1,0:T(8,128)S(1)} %get-tuple-element.13.refs_0_, f32[64,1024]{1,0:T(8,128)S(1)} %get-tuple-element.14.refs_1_, f32[64,128]{1,0:T(8,128)S(1)} %get-tuple-element.15.refs_2_, f32[64,128]{1,0:T(8,128)S(1)} %get-tuple-element.16.refs_3_), custom_call_target="tpu_custom_call" | custom-call | tf_op jit(solution)/shard_map/pallas_call | solution.py:342
  57.2 0.0 copy-start
  57.2 2.2 %copy-done = bf16[32,64,1024]{2,1,0:T(8,128)(2,1)S(1)} copy-done((bf16[32,64,1024]{2,1,0:T(8,128)(2,1)S(1)}, bf16[32,64,1024]{2,1,0:T(8,128)(2,1)}, u32[]{:S(2)}) %copy-start) | copy-done | bytes 4194328
  59.4 7.4 %shard_map.84 = f32[32,64,1024]{2,1,0:T(8,128)} custom-call(bf16[32,64,1024]{2,1,0:T(8,128)(2,1)S(1)} %copy-done, f32[32,64,128]{2,1,0:T(8,128)S(1)} %get-tuple-element.12.refs_1_, f32[128,1024]{1,0:T(8,128)S(1)} %shard_map.83.refs_2_), custom_call_target="tpu_custom_call" | custom-call | tf_op jit(solution)/shard_map/pallas_call | solution.py:371
  (1 shorter events, 0.0 us)
Async XLA Ops:
  2.1 0.7 %copy-start.1 = (s32[32,96]{1,0:T(8,128)S(1)}, s32[32,96]{1,0:T(8,128)}, u32[]{:S(2)}) copy-start(s32[32,96]{1,0:T(8,128)} %refs_2_.1) | copy-start | bytes 36868
  2.8 0.7 %copy-start.2 = (f32[4,64]{1,0:T(4,128)S(1)}, f32[4,64]{1,0:T(4,128)}, u32[]{:S(2)}) copy-start(f32[4,64]{1,0:T(4,128)} %refs_4_.1) | copy-start | bytes 3076
  3.5 0.7 copy-start.3
  57.2 2.2 %copy-start = (bf16[32,64,1024]{2,1,0:T(8,128)(2,1)S(1)}, bf16[32,64,1024]{2,1,0:T(8,128)(2,1)}, u32[]{:S(2)}) copy-start(bf16[32,64,1024]{2,1,0:T(8,128)(2,1)} %get-tuple-element.11.refs_0_) | copy-start | bytes 12582916
